TPU v7x, 128 devices: a whole 4x4x4 slice. The times are simulated.
128 devices in a mesh: row: 16 (over x, z_lo, core), col: 8 (over y, z_hi).
Axes of the slice: x: 4, y: 4, z: 4 (z_hi: 2, z_lo: 2; z = z_hi * 2 + z_lo), core: 2. Of those that a mesh axis runs over, the one named last changes fastest.
Arguments:
- density: bfloat16 [8192, 8192], P('row', 'col'), may hold values from -0.0625 to 0.0625
- intersection: bfloat16 [8192, 8192], P('row', 'col'), may hold values from -12 to 12
- density_mask: int32 [64, 64], P('row', 'col'), may hold values 0 or 1
- intersection_mask: int32 [64, 64], P('row', 'col'), may hold values 0 or 1
- filter_mask: int32 [64, 64], P('row', 'col'), may hold values 0 or 1
Outputs:
- psp: bfloat16 [8192, 8192], P('row', 'col')
- electrons: float32 [], replicated
All inputs are finite; a program needn't handle non-finite values. No bound on the sum of `density_mask` or of `intersection_mask` or of `filter_mask` on one device may be relied on, other than what follows from the above.
Results may differ from a plain program's by a relative error of at most 0.0049.
Values may be sent and summed in bfloat16 or wider, within the bound.
A program may use at most 128 MiB of HBM per device.

v0:
```python
import jax
import jax.numpy as jnp
from jax import lax
from jax.sharding import PartitionSpec as P

BLOCK = 128


def apply_mask(values, mask):
    rows = mask.shape[0]
    cols = mask.shape[1]
    shaped = values.reshape(rows, BLOCK, cols, BLOCK)
    return (shaped * mask.astype(values.dtype)[:, None, :, None]).reshape(values.shape)


def shards(density, intersection, density_mask, intersection_mask, filter_mask):
    left = apply_mask(density, density_mask)
    right = apply_mask(intersection, intersection_mask)
    height = left.shape[0]
    width = left.shape[1]
    over_panel = lax.all_gather(right, "row", axis=0, tiled=True)
    rows_part = over_panel
    product = jnp.dot(
        lax.all_gather(left, "col", axis=1, tiled=True),
        rows_part,
        preferred_element_type=jnp.float32,
    )
    first_row = lax.axis_index("row") * height
    first_col = lax.axis_index("col") * width
    row_ids = first_row + lax.broadcasted_iota(jnp.int32, (height, width), 0)
    col_ids = first_col + lax.broadcasted_iota(jnp.int32, (height, width), 1)
    diagonal = jnp.sum(jnp.where(row_ids == col_ids, product, 0.0))
    electrons = lax.psum(diagonal, ("row", "col"))
    filtered = apply_mask(product, filter_mask).astype(jnp.bfloat16)
    dens_panel_cols = lax.all_gather(left, "row", axis=0, tiled=True)
    rows_part = dens_panel_cols
    result = jnp.dot(
        lax.all_gather(filtered, "col", axis=1, tiled=True),
        rows_part,
        preferred_element_type=jnp.float32,
    )
    psp = apply_mask(result, filter_mask).astype(jnp.bfloat16)
    return (psp, electrons)


def solution(mesh):
    placed = (P("row", "col"), P("row", "col"), P("row", "col"), P("row", "col"), P("row", "col"))
    return jax.shard_map(
        shards, mesh=mesh, in_specs=placed, out_specs=(P("row", "col"), P()), check_vma=False
    )
```

profile of v0, /device:TPU:0, one launch (start us, length us, event | category | flops | bytes accessed | tf_op | source)
XLA Modules:
  0.0 444.1 jit_solution(4201503022961974298)
XLA Ops:
  7.2 0.0 copy-start
  7.2 0.0 all-gather.5.cloned.1.call-start
  7.2 0.7 convert_element_type.16
  7.9 0.2 mul.46
  8.1 2.3 bitcast_multiply_fusion.3
  10.5 0.0 all-gather.5.cloned.1.call-update
  10.5 0.0 all-gather.7.cloned.1.call-start
  10.5 0.7 convert_element_type.17
  11.2 0.2 mul.49
  11.4 2.3 bitcast_multiply_fusion.2
  13.8 0.0 all-gather.7.cloned.1.call-update
  13.8 0.0 all-gather.11.cloned.1.call-start
  13.8 0.7 all-gather.11.cloned.1.call-update
  14.5 0.0 all-gather.9.cloned.1.call-start
  14.6 0.0 copy-done
  14.6 107.8 %all-gather.5.cloned.1.call-done = bf16[512,8192]{1,0:T(8,128)(2,1)} async-done(((bf16[512,1024]{1,0:T(8,128)(2,1)}), bf16[512,8192]{1,0:T(8,128)(2,1)}) %all-gather.5.cloned.1.call-update) | async-done | bytes 8388624 | tf_op jit(solution)/shard_map/all_gather | solution.py:24
  122.4 91.1 %all-gather.7.cloned.1.call-done = bf16[8192,1024]{1,0:T(8,128)(2,1)} async-done(((bf16[512,1024]{1,0:T(8,128)(2,1)}), bf16[8192,1024]{1,0:T(8,128)(2,1)}) %all-gather.7.cloned.1.call-update) | async-done | bytes 16777232 | tf_op jit(solution)/shard_map/all_gather | solution.py:21
  213.5 0.2 mul.52
  213.7 16.6 %select_reduce_fusion = (f32[]{:T(128)}, bf16[512,1024]{1,0:T(8,128)(2,1)}) fusion(s32[1024]{0:T(1024)S(1)} %iota_add_fusion, s32[512]{0:T(512)S(1)} %iota_add_fusion.1, f32[64,8,8,128]{3,2,1,0:T(8,128)S(1)} %bitcast.23, bf16[512,8192]{1,0:T(8,128)(2,1)} %all-gather.5.cloned.1.call-done, bf16[8192,1024]{1,0:T(8,128)(2,1)} %all-gather.7.cloned.1.call-done), kind=kOutput, calls=%fused_computation.4 | convolution fusion | flops 8592556032 | bytes 28317700 | tf_op jit(solution)/shard_map/dot_general | solution.py:23
  230.3 0.0 all-gather.9.cloned.1.call-update
  230.3 66.2 %psum.7 = f32[]{:T(128)} all-reduce(f32[]{:T(128)} %get-tuple-element.2), channel_id=1, replica_groups=mesh['row'=16,'col'=8] {'row','col'}, use_global_device_ids=true, to_apply=%region_1.2 | all-reduce | flops 1 | bytes 8 | tf_op jit(solution)/shard_map/psum | solution.py:33
  296.6 13.0 %all-gather.11.cloned.1.call-done = bf16[8192,1024]{1,0:T(8,128)(2,1)} async-done(((bf16[512,1024]{1,0:T(8,128)(2,1)}), bf16[8192,1024]{1,0:T(8,128)(2,1)}) %all-gather.11.cloned.1.call-update) | async-done | bytes 16777232 | tf_op jit(solution)/shard_map/all_gather | solution.py:35
  309.6 112.2 %all-gather.9.cloned.1.call-done = bf16[512,8192]{1,0:T(8,128)(2,1)} async-done(((bf16[512,1024]{1,0:T(8,128)(2,1)}), bf16[512,8192]{1,0:T(8,128)(2,1)}) %all-gather.9.cloned.1.call-update) | async-done | bytes 8388624 | tf_op jit(solution)/shard_map/all_gather | solution.py:38
  421.8 15.8 %fusion.1 = bf16[512,1024]{1,0:T(8,128)(2,1)} fusion(f32[64,8,8,128]{3,2,1,0:T(8,128)S(1)} %bitcast.24, bf16[512,8192]{1,0:T(8,128)(2,1)} %all-gather.9.cloned.1.call-done, bf16[8192,1024]{1,0:T(8,128)(2,1)} %all-gather.11.cloned.1.call-done), kind=kOutput, calls=%fused_computation.3 | convolution fusion | flops 8590983168 | bytes 28311552 | tf_op jit(solution)/shard_map/dot_general | solution.py:37
  (3 shorter events, 0.0 us)
Async XLA Ops:
  7.2 7.4 %copy-start = (s32[4,8]{1,0:T(4,128)S(1)}, s32[4,8]{1,0:T(4,128)}, u32[]{:S(2)}) copy-start(s32[4,8]{1,0:T(4,128)} %param.9) | copy-start | bytes 388
  7.2 115.2 %all-gather.5.cloned.1.call-start = ((), (), s32[]{:S(2)}) async-start(), calls=%async_computation | async-start | bytes 9437184 | tf_op jit(solution)/shard_map/all_gather | solution.py:24
  10.5 203.0 %all-gather.7.cloned.1.call-start = ((), (), s32[]{:S(2)}) async-start(), calls=%async_computation.1 | async-start | bytes 17825792 | tf_op jit(solution)/shard_map/all_gather | solution.py:21
  13.8 295.8 %all-gather.11.cloned.1.call-start = ((), (), s32[]{:S(2)}) async-start(), calls=%async_computation.3 | async-start | bytes 17825792 | tf_op jit(solution)/shard_map/all_gather | solution.py:35
  14.5 407.2 %all-gather.9.cloned.1.call-start = ((), (), s32[]{:S(2)}) async-start(), calls=%async_computation.2 | async-start | bytes 9437184 | tf_op jit(solution)/shard_map/all_gather | solution.py:38
Sparse Core Ops, SparseCore 0:
  10.9 111.4 all-gather.4
  124.1 89.3 all-gather.6
  215.8 93.7 all-gather.10
  311.8 109.9 all-gather.8
where the time goes:
time: 445 us; the launch traced here: 444 us
  waiting for transfers between devices  325 us (73%)
  blocking collectives  66.2 us (15%)
  matrix products  32.4 us (7%)
  between operations  13.8 us (3%)
  other arithmetic  6.05 us (1%)
    all_gather x1, waiting for transfers between devices, shards(): lax.all_gather(filtered, 'col', axis=1, tiled=True)  112 us
    all_gather x1, waiting for transfers between devices, shards(): lax.all_gather(left, 'col', axis=1, tiled=True)  108 us
    all_gather x1, waiting for transfers between devices, shards(): over_panel = lax.all_gather(right, 'row', axis=0, tiled=True)  91.1 us
    psum x1, blocking collectives, shards(): electrons = lax.psum(diagonal, ('row', 'col'))  66.2 us
    dot_general x1, matrix products, shards(): jnp.dot(lax.all_gather(left, 'col', axis=1, tiled=True), rows_part, prefe...  16.6 us
    dot_general x1, matrix products, shards(): jnp.dot(lax.all_gather(filtered, 'col', axis=1, tiled=True), rows_part, p...  15.8 us
    all_gather x1, waiting for transfers between devices, shards(): dens_panel_cols = lax.all_gather(left, 'row', axis=0, tiled=True)  13 us
  transfers between devices with their start and end apart: 4, of which 4 were waited for; matrix products, arithmetic and copies ran while one was open for 5% of the time, Pallas kernels for 0%

commit v1 on v0

v1 whole, which is shorter than its diff:
```python
import jax
import jax.numpy as jnp
from jax import lax
from jax.experimental import pallas as pl
from jax.experimental.pallas import tpu as pltpu
from jax.sharding import PartitionSpec as P

BLOCK = 128
ROWS = 512
COLS = 1024
CHUNK = 128
HALF = 256
NTILE = 256
MESH = pl.DeviceIdType.MESH


def kernel(
    dm_ref, im_ref, fm_ref, p_ref, s_ref, o_ref, e_ref,
    pz, a1, s1, b2, fa, acc1, acc2, r1s, r1r, r2s, r2r, eb,
    zs, zr, zfs, zfr, ys, yr, yfs, yfr, ss, sr, sfs, sfr, sds, sdr,
    bs, br, bfs, bfr, bds, bdr, r1ss, r1rs, fs, fr, ffs, ffr, r2ss, r2rs, es, er,
):
    row = lax.axis_index("row")
    col = lax.axis_index("col")
    core = lax.rem(row, 2)
    zl = lax.rem(row // 2, 2)
    x = row // 4
    zh = lax.rem(col, 2)
    y = col // 2
    z = 2 * zh + zl

    def wrap(v):
        return lax.rem(v + 4, 4)

    def dev(x_=x, y_=y, z_=z, c_=core):
        return {"row": x_ * 4 + lax.rem(z_, 2) * 2 + c_, "col": y_ * 2 + z_ // 2}

    xs = [dev(x_=wrap(x + 1)), dev(x_=wrap(x - 1))]
    yd = [dev(y_=wrap(y + 1)), dev(y_=wrap(y - 1))]
    zd = [dev(z_=wrap(z + 1)), dev(z_=wrap(z - 1))]
    x2, y2, z2 = dev(x_=wrap(x + 2)), dev(y_=wrap(y + 2)), dev(z_=wrap(z + 2))
    zp = dev(z_=2 * zh + 1 - zl)
    mate = dev(c_=1 - core)
    xfrom = [wrap(x - 1), wrap(x + 1)]
    zfrom = [wrap(z - 1), wrap(z + 1)]

    peers = xs + yd + zd + [x2, y2, z2, mate]
    barrier = pltpu.get_barrier_semaphore()
    for d in peers:
        pl.semaphore_signal(barrier, inc=1, device_id=d, device_id_type=MESH)
    pl.semaphore_wait(barrier, len(peers))

    sent = []

    def copy(src, dst, ssem, rsem, device):
        return pltpu.make_async_remote_copy(
            src_ref=src, dst_ref=dst, send_sem=ssem, recv_sem=rsem,
            device_id=device, device_id_type=MESH,
        )

    def send(src, dst, ssem, rsem, device):
        cp = copy(src, dst, ssem, rsem, device)
        cp.start()
        sent.append(cp)

    def arrived(ref, ssem, rsem):
        copy(ref, ref, ssem, rsem, mate).wait_recv()

    def rows(j, n=CHUNK):
        return pl.ds(j * n, n)

    def blocks_masked(val, mask_ref, i):
        parts = []
        for b in range(COLS // BLOCK):
            keep = jnp.full((BLOCK, BLOCK), mask_ref[i, b], jnp.int32) != 0
            part = val[:, b * BLOCK:(b + 1) * BLOCK].astype(jnp.float32)
            parts.append(jnp.where(keep, part, 0.0))
        return jnp.concatenate(parts, axis=1).astype(jnp.bfloat16)

    n1, k1 = 1 + zl, 1 - zl
    n2, k2 = 3 * zl, zl

    def send_a(n, k, kk, j):
        src = pz.at[n, rows(j)]
        for d in range(2):
            send(src, a1.at[d, k, rows(j)], ys.at[d, kk, j], yr.at[d, k, j], yd[d])

    own_in_a = zh == zl

    for j in range(4):
        pz[z, rows(j)] = blocks_masked(p_ref[rows(j)], dm_ref, j)
        src = pz.at[z, rows(j)]
        for d in range(2):
            send(src, src, zs.at[d, j], zr.at[d, j], zd[d])
        if j < 2:
            src_y = pz.at[n2, rows(j)]

            @pl.when(own_in_a)
            def _():
                for d in range(2):
                    copy(src_y, a1.at[d, k2, rows(j)], ys.at[d, 1, j], yr.at[d, k2, j], yd[d]).start()

    def s_piece(xx, cc, h):
        return s1.at[xx, pl.ds(pl.multiple_of(cc * ROWS + h * HALF, HALF), HALF)]

    for h in range(2):
        for i in range(2):
            j = 2 * h + i
            s1[x, pl.ds(pl.multiple_of(core * ROWS + j * CHUNK, CHUNK), CHUNK)] = blocks_masked(
                s_ref[rows(j)], im_ref, j)
        src = s_piece(x, core, h)
        for d in range(2):
            send(src, src, ss.at[d, h], sr.at[d, h], xs[d])
        send(src, src, sds.at[0, h], sdr.at[0, h], mate)

    def z_step(j):
        for d in range(2):
            arrived(pz.at[zfrom[d], rows(j)], zs.at[d, j], zr.at[d, j])
        d = j % 2
        src = pz.at[zfrom[d], rows(j)]
        send(src, src, zfs.at[j], zfr.at[j], zd[d])
        send_a(n1, k1, 0, j)

    def z_opp(j):
        arrived(pz.at[wrap(z + 2), rows(j)], zfs.at[j], zfr.at[j])

    def s_step(h):
        for d in range(2):
            src = s_piece(xfrom[d], core, h)
            arrived(src, ss.at[d, h], sr.at[d, h])
            if d == h:
                send(src, src, sfs.at[h], sfr.at[h], xs[d])
            send(src, src, sds.at[1 + d, h], sdr.at[1 + d, h], mate)

    def s_opp(h):
        src = s_piece(wrap(x + 2), core, h)
        arrived(src, sfs.at[h], sfr.at[h])
        send(src, src, sds.at[3, h], sdr.at[3, h], mate)

    def s_mate(i, h):
        xx = [x, xfrom[0], xfrom[1], wrap(x + 2)][i]
        arrived(s_piece(xx, 1 - core, h), sds.at[i, h], sdr.at[i, h])

    z_step(0)
    z_step(1)
    s_step(0)
    for j in (2, 3):
        src = pz.at[n2, rows(j)]

        @pl.when(own_in_a)
        def _():
            for d in range(2):
                copy(src, a1.at[d, k2, rows(j)], ys.at[d, 1, j], yr.at[d, k2, j], yd[d]).start()

    def late_n2(j):
        z_opp(j)
        src = pz.at[n2, rows(j)]
        cps = [copy(src, a1.at[d, k2, rows(j)], ys.at[d, 1, j], yr.at[d, k2, j], yd[d]) for d in range(2)]

        @pl.when(jnp.logical_not(own_in_a))
        def _():
            for cp in cps:
                cp.start()

        sent.extend(cps)

    late_n2(0)
    late_n2(1)
    z_step(2)
    z_step(3)
    s_step(1)
    late_n2(2)
    late_n2(3)

    def b_piece(t, xx, cc, h):
        return b2.at[t, xx, pl.ds(pl.multiple_of(cc * ROWS + h * HALF, HALF), HALF)]

    tile = [2 - zh, 3 * zh]

    def b_start(t):
        for h in range(2):
            src = pz.at[tile[t], rows(h, HALF)]
            for d in range(2):
                send(src, b_piece(t, x, core, h), bs.at[t, d, h], br.at[t, d, h], xs[d])
            send(src, b_piece(t, x, core, h), bds.at[t, 0, h], bdr.at[t, 0, h], mate)
            b2[t, x, pl.ds(pl.multiple_of(core * ROWS + h * HALF, HALF), HALF)] = pz[tile[t], rows(h, HALF)]

    def b_step(t, h):
        for d in range(2):
            src = b_piece(t, xfrom[d], core, h)
            arrived(src, bs.at[t, d, h], br.at[t, d, h])
            if d == h:
                send(src, src, bfs.at[t, h], bfr.at[t, h], xs[d])
            send(src, src, bds.at[t, 1 + d, h], bdr.at[t, 1 + d, h], mate)

    def b_opp(t, h):
        src = b_piece(t, wrap(x + 2), core, h)
        arrived(src, bfs.at[t, h], bfr.at[t, h])
        send(src, src, bds.at[t, 3, h], bdr.at[t, 3, h], mate)

    def b_mate(t, i, h):
        xx = [x, xfrom[0], xfrom[1], wrap(x + 2)][i]
        arrived(b_piece(t, xx, 1 - core, h), bds.at[t, i, h], bdr.at[t, i, h])

    def a_forward(j):
        for d in range(2):
            for k in range(2):
                arrived(a1.at[d, k, rows(j)], ys.at[d, k, j], yr.at[d, k, j])
            src = a1.at[d, d, rows(j)]
            send(src, a1.at[2, d, rows(j)], yfs.at[d, j], yfr.at[d, j], yd[d])

    def a_opp(j):
        for d in range(2):
            arrived(a1.at[2, d, rows(j)], yfs.at[d, j], yfr.at[d, j])

    def ncols(n):
        return pl.ds(pl.multiple_of(n * NTILE, NTILE), NTILE)

    def m1_own(h):
        @pl.loop(0, COLS // NTILE)
        def _(n):
            for k in range(2):
                acc1[k, rows(h, HALF), ncols(n)] = jnp.dot(
                    pz[2 * zl + k, rows(h, HALF)], s1[y, :, ncols(n)], preferred_element_type=jnp.float32)

    def m1(slot, yy, h):
        @pl.loop(0, COLS // NTILE)
        def _(n):
            for k in range(2):
                acc1[k, rows(h, HALF), ncols(n)] += jnp.dot(
                    a1[slot, k, rows(h, HALF)], s1[yy, :, ncols(n)], preferred_element_type=jnp.float32)

    yrel = [wrap(y - 1), wrap(y + 1), wrap(y + 2)]

    def rs1_start(h):
        for j in (2 * h, 2 * h + 1):
            r1s[rows(j)] = acc1[1 - zl, rows(j)].astype(jnp.bfloat16)
            send(r1s.at[rows(j)], r1r.at[rows(j)], r1ss.at[j], r1rs.at[j], zp)

    def f_start(j):
        arrived(r1r.at[rows(j)], r1ss.at[j], r1rs.at[j])
        total = acc1[zl, rows(j)] + r1r[rows(j)].astype(jnp.float32)
        fa[0, rows(j)] = blocks_masked(total, fm_ref, j)
        for d in range(2):
            send(fa.at[0, rows(j)], fa.at[1 + d, rows(j)], fs.at[d, j], fr.at[d, j], yd[d])

    def f_forward(j):
        for d in range(2):
            arrived(fa.at[1 + d, rows(j)], fs.at[d, j], fr.at[d, j])
        d = j % 2
        send(fa.at[1 + d, rows(j)], fa.at[3, rows(j)], ffs.at[j], ffr.at[j], yd[d])

    def f_opp(j):
        arrived(fa.at[3, rows(j)], ffs.at[j], ffr.at[j])

    def diagonal(h):
        at = pl.multiple_of(core * ROWS + h * HALF, HALF)
        square = acc1[zh, rows(h, HALF), pl.ds(at, HALF)]
        r = lax.broadcasted_iota(jnp.int32, (HALF, HALF), 0)
        c = lax.broadcasted_iota(jnp.int32, (HALF, HALF), 1)
        return jnp.sum(jnp.where(r == c, square, 0.0))

    stages = [
        (core, 2, lambda i: dev(c_=lax.rem(core + i, 2))),
        (z, 4, lambda i: dev(z_=lax.rem(z + i, 4))),
        (y, 4, lambda i: dev(y_=lax.rem(y + i, 4))),
        (x, 4, lambda i: dev(x_=lax.rem(x + i, 4))),
    ]

    def e_send(st):
        me, n, target = stages[st]
        for i in range(1, n):
            send(eb.at[st, me], eb.at[st, me], es.at[st, i], er.at[st, i], target(i))

    def e_sum(st):
        me, n, _ = stages[st]
        for i in range(1, n):
            arrived(eb.at[st, lax.rem(me + n - i, n)], es.at[st, i], er.at[st, i])
        total = eb[st, 0]
        for i in range(1, n):
            total = total + eb[st, i]
        return total

    def e_step(st):
        total = e_sum(st)
        eb[st + 1, stages[st + 1][0]] = total
        e_send(st + 1)

    b_start(0)
    s_opp(0)
    s_opp(1)
    b_start(1)
    a_forward(0)
    a_forward(1)
    for i in range(4):
        for h in range(2):
            s_mate(i, h)
    m1_own(0)
    m1(0, yrel[0], 0)
    m1(1, yrel[1], 0)
    a_opp(0)
    a_opp(1)
    m1(2, yrel[2], 0)
    rs1_start(0)
    trace = diagonal(0)
    for h in range(2):
        b_step(0, h)
    m1_own(1)
    a_forward(2)
    a_forward(3)
    f_start(0)
    f_start(1)
    m1(0, yrel[0], 1)
    m1(1, yrel[1], 1)
    for h in range(2):
        b_opp(0, h)
    a_opp(2)
    a_opp(3)
    m1(2, yrel[2], 1)
    rs1_start(1)
    trace = trace + diagonal(1)
    trace = jnp.where(x == y, trace, 0.0)
    eb[0, core] = jnp.full((8, 128), trace, jnp.float32)
    e_send(0)
    f_forward(0)
    f_forward(1)
    f_start(2)
    f_start(3)
    e_step(0)

    def m2(t, slot, yy, start, size, first):
        span = pl.ds(start, size)

        @pl.loop(0, COLS // NTILE)
        def _(n):
            d = jnp.dot(fa[slot, span], b2[t, yy, :, ncols(n)], preferred_element_type=jnp.float32)
            if first:
                acc2[t, span, ncols(n)] = d
            else:
                acc2[t, span, ncols(n)] += d

    def rs2_start(j):
        r2s[rows(j)] = acc2[0, rows(j)].astype(jnp.bfloat16)
        send(r2s.at[rows(j)], r2r.at[rows(j)], r2ss.at[j], r2rs.at[j], z2)

    for i in range(4):
        for h in range(2):
            b_mate(0, i, h)
    f_opp(0)
    f_opp(1)
    m2(0, 0, y, 0, HALF, True)
    for i in range(3):
        m2(0, 1 + i, yrel[i], 0, HALF, False)
    rs2_start(0)
    rs2_start(1)
    e_step(1)
    m2(0, 0, y, HALF, HALF, True)
    for h in range(2):
        b_step(1, h)
    e_step(2)
    f_forward(2)
    f_forward(3)
    for i in range(2):
        m2(0, 1 + i, yrel[i], HALF, HALF, False)
    for h in range(2):
        b_opp(1, h)
    for j in (2, 3):
        f_opp(j)
        m2(0, 3, yrel[2], j * CHUNK, CHUNK, False)
        rs2_start(j)
    for i in range(4):
        for h in range(2):
            b_mate(1, i, h)
    m2(1, 0, y, 0, ROWS, True)
    for i in range(3):
        m2(1, 1 + i, yrel[i], 0, ROWS, False)
    e_ref[...] = e_sum(3)
    for j in range(4):
        arrived(r2r.at[rows(j)], r2ss.at[j], r2rs.at[j])
        total = acc2[1, rows(j)] + r2r[rows(j)].astype(jnp.float32)
        o_ref[rows(j)] = blocks_masked(total, fm_ref, j)
    for cp in sent:
        cp.wait_send()


def shards(density, intersection, density_mask, intersection_mask, filter_mask):
    dma = pltpu.SemaphoreType.DMA
    bf16, f32 = jnp.bfloat16, jnp.float32
    vmem, smem = pl.BlockSpec(memory_space=pltpu.VMEM), pl.BlockSpec(memory_space=pltpu.SMEM)
    psp, electrons = pl.pallas_call(
        kernel,
        out_shape=(jax.ShapeDtypeStruct((ROWS, COLS), bf16), jax.ShapeDtypeStruct((8, 128), f32)),
        in_specs=[smem] * 3 + [vmem] * 2,
        out_specs=(vmem, vmem),
        scratch_shapes=[
            pltpu.VMEM((4, ROWS, COLS), bf16),
            pltpu.VMEM((3, 2, ROWS, COLS), bf16),
            pltpu.VMEM((4, 2 * ROWS, COLS), bf16),
            pltpu.VMEM((2, 4, 2 * ROWS, COLS), bf16),
            pltpu.VMEM((4, ROWS, COLS), bf16),
            pltpu.VMEM((2, ROWS, COLS), f32),
            pltpu.VMEM((2, ROWS, COLS), f32),
            pltpu.VMEM((ROWS, COLS), bf16),
            pltpu.VMEM((ROWS, COLS), bf16),
            pltpu.VMEM((ROWS, COLS), bf16),
            pltpu.VMEM((ROWS, COLS), bf16),
            pltpu.VMEM((4, 4, 8, 128), f32),
            dma((2, 4)), dma((2, 4)), dma((4,)), dma((4,)),
            dma((2, 2, 4)), dma((2, 2, 4)), dma((2, 4)), dma((2, 4)),
            dma((2, 2)), dma((2, 2)), dma((2,)), dma((2,)), dma((4, 2)), dma((4, 2)),
            dma((2, 2, 2)), dma((2, 2, 2)), dma((2, 2)), dma((2, 2)), dma((2, 4, 2)), dma((2, 4, 2)),
            dma((4,)), dma((4,)),
            dma((2, 4)), dma((2, 4)), dma((4,)), dma((4,)),
            dma((4,)), dma((4,)),
            dma((4, 4)), dma((4, 4)),
        ],
        compiler_params=pltpu.CompilerParams(
            collective_id=0, has_side_effects=True, vmem_limit_bytes=62 * 2**20
        ),
        cost_estimate=pl.CostEstimate(flops=17179869184, bytes_accessed=3 * 2**20, transcendentals=0),
    )(density_mask, intersection_mask, filter_mask, density, intersection)
    return psp, electrons[0, 0]


def solution(mesh):
    placed = (P("row", "col"),) * 5
    return jax.shard_map(
        shards, mesh=mesh, in_specs=placed, out_specs=(P("row", "col"), P()), check_vma=False
    )
```

time: 445 us -> 156 us (0.35)
  waiting for transfers between devices: 325 us -> 0 us
  Pallas kernels: 0 us -> 152 us
  blocking collectives: 66.2 us -> 0 us
  matrix products: 32.4 us -> 0 us
  between operations: 13.8 us -> 0.64 us
  other arithmetic: 6.05 us -> 0 us
    all_gather x4 -> x0, waiting for transfers between devices: 324 us -> none  [the longest x1 112 us: shards(): lax.all_gather(filtered, 'col', axis=1, tiled=True)]
    pallas_call x0 -> x1, Pallas kernels: none -> 152 us  [shards(): pl.pallas_call(kernel, out_shape=(jax.ShapeDtypeStruct((ROWS, COLS), bf16...]
    psum x1 -> x0, blocking collectives: 66.2 us -> none  [shards(): electrons = lax.psum(diagonal, ('row', 'col'))]
    dot_general x2 -> x0, matrix products: 32.4 us -> none  [the longest x1 16.6 us: shards(): jnp.dot(lax.all_gather(left, 'col', axis=1, tiled=True), rows_part, prefe...]
    mul x2 -> x0, other arithmetic: 4.67 us -> none  [apply_mask(): shaped * mask.astype(values.dtype)[:, None, :, None]]
  transfers between devices with their start and end apart: 4 -> 0, of which waited for: 4 -> 0; matrix products, arithmetic and copies ran while one was open for 5% -> 0% of each run, Pallas kernels for 0% -> 0%
where the time goes in v1:
time: 156 us
  Pallas kernels  152 us (97%)
  local copies, waits for them, and re-layouts  3.45 us (2%)
    pallas_call x1, Pallas kernels, shards(): pl.pallas_call(kernel, out_shape=(jax.ShapeDtypeStruct((ROWS, COLS), bf16...  152 us

profile of v1, /device:TPU:0, one launch (start us, length us, event | category | flops | bytes accessed | tf_op | source)
XLA Modules:
  0.0 156.0 jit_solution(10985943820394591600)
XLA Ops:
  0.6 151.9 %shard_map.68 = (bf16[512,1024]{1,0:T(8,128)(2,1)}, f32[8,128]{1,0:T(8,128)}) custom-call(s32[4,8]{1,0:T(4,128)} %dm_ref.1, s32[4,8]{1,0:T(4,128)} %im_ref.1, s32[4,8]{1,0:T(4,128)} %fm_ref.1, bf16[512,1024]{1,0:T(8,128)(2,1)} %p_ref.1, bf16[512,1024]{1,0:T(8,128)(2,1)} %s_ref.1), custom_call_target="tpu_custom_call" | custom-call | flops 17179869184 | bytes 3145728 | tf_op jit(solution)/shard_map/pallas_call | solution.py:390
  152.5 1.2 slice.3
  153.7 2.3 %copy.8 = bf16[512,1024]{1,0:T(8,128)(2,1)} copy(bf16[512,1024]{1,0:T(8,128)(2,1)} %get-tuple-element.8) | data formatting | bytes 2097152

commit v2 on v1

v2 whole, which is shorter than its diff:
```python
import jax
import jax.numpy as jnp
from jax import lax
from jax.experimental import pallas as pl
from jax.experimental.pallas import tpu as pltpu
from jax.sharding import PartitionSpec as P

BLOCK = 128
ROWS = 512
COLS = 1024
CHUNK = 128
HALF = 256
NTILE = 256
MESH = pl.DeviceIdType.MESH


def kernel(
    dm_ref, im_ref, fm_ref, p_ref, s_ref, o_ref, e_ref,
    pz, yb, yf, a1, s1, b2, fa, acc1, acc2, r1s, r1r, r2s, r2r, eb,
    zs, zr, zfs, zfr, ys, yr, yfs, yfr, ybs, ybr, yzs, yzr, ss, sr, sfs, sfr, sds, sdr,
    bs, br, bfs, bfr, bds, bdr, r1ss, r1rs, fs, fr, ffs, ffr, r2ss, r2rs, es, er,
):
    row = lax.axis_index("row")
    col = lax.axis_index("col")
    core = lax.rem(row, 2)
    zl = lax.rem(row // 2, 2)
    x = row // 4
    zh = lax.rem(col, 2)
    y = col // 2
    z = 2 * zh + zl

    def wrap(v):
        return lax.rem(v + 4, 4)

    def dev(x_=x, y_=y, z_=z, c_=core):
        return {"row": x_ * 4 + lax.rem(z_, 2) * 2 + c_, "col": y_ * 2 + z_ // 2}

    xs = [dev(x_=wrap(x + 1)), dev(x_=wrap(x - 1))]
    yd = [dev(y_=wrap(y + 1)), dev(y_=wrap(y - 1))]
    zd = [dev(z_=wrap(z + 1)), dev(z_=wrap(z - 1))]
    x2, y2, z2 = dev(x_=wrap(x + 2)), dev(y_=wrap(y + 2)), dev(z_=wrap(z + 2))
    zp = dev(z_=2 * zh + 1 - zl)
    mate = dev(c_=1 - core)
    xfrom = [wrap(x - 1), wrap(x + 1)]

    peers = xs + yd + zd + [x2, y2, z2, mate]
    barrier = pltpu.get_barrier_semaphore()
    for d in peers:
        pl.semaphore_signal(barrier, inc=1, device_id=d, device_id_type=MESH)
    pl.semaphore_wait(barrier, len(peers))

    sent = []

    def copy(src, dst, ssem, rsem, device):
        return pltpu.make_async_remote_copy(
            src_ref=src, dst_ref=dst, send_sem=ssem, recv_sem=rsem,
            device_id=device, device_id_type=MESH,
        )

    def send(src, dst, ssem, rsem, device):
        cp = copy(src, dst, ssem, rsem, device)
        cp.start()
        sent.append(cp)

    def arrived(ref, ssem, rsem):
        copy(ref, ref, ssem, rsem, mate).wait_recv()

    def rows(j, n=CHUNK):
        return pl.ds(j * n, n)

    def blocks_masked(val, mask_ref, i):
        parts = []
        for b in range(COLS // BLOCK):
            keep = jnp.full((BLOCK, BLOCK), mask_ref[i, b], jnp.int32) != 0
            part = val[:, b * BLOCK:(b + 1) * BLOCK].astype(jnp.float32)
            parts.append(jnp.where(keep, part, 0.0))
        return jnp.concatenate(parts, axis=1).astype(jnp.bfloat16)

    n1, k1 = 1 + zl, 1 - zl
    n2, k2 = 3 * zl, zl

    def send_a(n, k, kk, j):
        src = pz.at[n, rows(j)]
        for d in range(2):
            send(src, a1.at[d, k, rows(j)], ys.at[d, kk, j], yr.at[d, k, j], yd[d])

    own_in_a = zh == zl
    inside = zh != zl

    nl = jnp.where(own_in_a, 2 - zl, 3 - 3 * zl)

    def zdev(v):
        return dev(z_=v)

    def z_copies(j):
        src = pz.at[z, rows(j)]
        inner = [
            copy(src, src, zs.at[0, j], zr.at[0, j], zdev(3 - z)),
            copy(src, src, zs.at[1, j], zr.at[0, j], zdev(nl)),
        ]
        outer = copy(src, src, zs.at[0, j], zr.at[1, j], zdev(n1))
        return inner, outer

    def z_start(j):
        inner, outer = z_copies(j)

        @pl.when(own_in_a)
        def _():
            outer.start()

        @pl.when(inside)
        def _():
            for cp in inner:
                cp.start()

    def z_step(j):
        arrived(pz.at[n1, rows(j)], zs.at[0, j], zr.at[0, j])
        if j < 2:
            send_a(n1, k1, 0, j)

        @pl.when(inside)
        def _():
            arrived(pz.at[nl, rows(j)], zs.at[0, j], zr.at[1, j])

        src = pz.at[jnp.where(own_in_a, n1, nl), rows(j)]
        send(src, src, zfs.at[j], zfr.at[j], zdev(3 - z))

    def z_far(j):
        @pl.when(inside)
        def _():
            arrived(pz.at[n2, rows(j)], zfs.at[j], zfr.at[j])

    def z_late(j):
        @pl.when(own_in_a)
        def _():
            arrived(pz.at[nl, rows(j)], zfs.at[j], zfr.at[j])

    def z_sent(j):
        inner, outer = z_copies(j)

        @pl.when(own_in_a)
        def _():
            outer.wait_send()

        @pl.when(inside)
        def _():
            for cp in inner:
                cp.wait_send()

    def n2_copies(j):
        src = pz.at[n2, rows(j)]
        return [copy(src, a1.at[d, k2, rows(j)], ys.at[d, 1, j], yr.at[d, k2, j], yd[d]) for d in range(2)]

    def n2_own(j):
        @pl.when(own_in_a)
        def _():
            for cp in n2_copies(j):
                cp.start()

    def n2_far(j):
        @pl.when(inside)
        def _():
            arrived(pz.at[n2, rows(j)], zfs.at[j], zfr.at[j])
            for cp in n2_copies(j):
                cp.start()

        sent.extend(n2_copies(j))

    LAST = 3

    def yb_start():
        for d in range(2):
            send(pz.at[z, rows(LAST)], yb.at[d], ybs.at[d], ybr.at[d], yd[d])

    def yb_step():
        for d in range(2):
            arrived(yb.at[d], ybs.at[d], ybr.at[d])
        for d in range(2):
            part = pl.ds(d * (CHUNK // 2), CHUNK // 2)
            send(yb.at[d, part], yb.at[2, part], yfs.at[d, LAST], yfr.at[d, LAST], yd[d])

    def yb_opp():
        for d in range(2):
            part = pl.ds(d * (CHUNK // 2), CHUNK // 2)
            arrived(yb.at[2, part], yfs.at[d, LAST], yfr.at[d, LAST])

    def yz_copies(i):
        dst = a1.at[i, zl, rows(LAST)]
        near = [
            copy(yb.at[i], dst, yzs.at[0, i], yzr.at[0, i], zdev(3 - z)),
            copy(yb.at[i], dst, yzs.at[1, i], yzr.at[0, i], zdev(nl)),
        ]
        far = copy(yb.at[i], yf.at[i], yzs.at[0, i], yzr.at[1, i], zdev(3 - z))
        return near, far

    def yz_start_outer(i):
        @pl.when(own_in_a)
        def _():
            yz_copies(i)[1].start()
            a1[i, zl, rows(LAST)] = yb[i]

    def yz_start_inner(i):
        @pl.when(inside)
        def _():
            for cp in yz_copies(i)[0]:
                cp.start()

    def yz_pass(i):
        return copy(yf.at[i], a1.at[i, 1 - zl, rows(LAST)], yzs.at[1, i], yzr.at[1, i], zdev(n1))

    def yz_relay(i):
        @pl.when(own_in_a)
        def _():
            arrived(yf.at[i], yzs.at[0, i], yzr.at[1, i])
            yz_pass(i).start()

    def yz_arrived(i):
        arrived(a1.at[i, k1, rows(LAST)], yzs.at[0, i], yzr.at[0, i])

        @pl.when(inside)
        def _():
            arrived(a1.at[i, k2, rows(LAST)], yzs.at[0, i], yzr.at[1, i])

    def yz_sent(i):
        near, far = yz_copies(i)

        @pl.when(own_in_a)
        def _():
            far.wait_send()
            yz_pass(i).wait_send()

        @pl.when(inside)
        def _():
            for cp in near:
                cp.wait_send()

    def p_mask(j):
        pz[z, rows(j)] = blocks_masked(p_ref[rows(j)], dm_ref, j)

    p_mask(LAST)
    yb_start()
    p_mask(0)
    z_start(0)

    def s_piece(xx, cc, h):
        return s1.at[xx, pl.ds(pl.multiple_of(cc * ROWS + h * HALF, HALF), HALF)]

    for h in range(2):
        for i in range(2):
            j = 2 * h + i
            s1[x, pl.ds(pl.multiple_of(core * ROWS + j * CHUNK, CHUNK), CHUNK)] = blocks_masked(
                s_ref[rows(j)], im_ref, j)
        src = s_piece(x, core, h)
        for d in range(2):
            send(src, src, ss.at[d, h], sr.at[d, h], xs[d])
        send(src, src, sds.at[0, h], sdr.at[0, h], mate)

    def s_part(xx, h, d):
        return s1.at[xx, pl.ds(pl.multiple_of(core * ROWS + h * HALF + d * CHUNK, CHUNK), CHUNK)]

    def s_step(h):
        for d in range(2):
            src = s_piece(xfrom[d], core, h)
            arrived(src, ss.at[d, h], sr.at[d, h])
            part = s_part(xfrom[d], h, d)
            send(part, part, sfs.at[d, h], sfr.at[d, h], xs[d])
            send(src, src, sds.at[1 + d, h], sdr.at[1 + d, h], mate)

    def s_opp(h):
        for d in range(2):
            arrived(s_part(wrap(x + 2), h, d), sfs.at[d, h], sfr.at[d, h])
        src = s_piece(wrap(x + 2), core, h)
        send(src, src, sds.at[3, h], sdr.at[3, h], mate)

    def s_mate(i, h):
        xx = [x, xfrom[0], xfrom[1], wrap(x + 2)][i]
        arrived(s_piece(xx, 1 - core, h), sds.at[i, h], sdr.at[i, h])

    tile = [2 - zh, 3 * zh]

    def b_rows(p, xx, cc, off=0, n=HALF):
        return b2.at[p // 2, xx, pl.ds(pl.multiple_of(cc * ROWS + (p % 2) * HALF + off, n), n)]

    def b_start(p):
        src, dst = pz.at[tile[p // 2], rows(p % 2, HALF)], b_rows(p, x, core)
        for d in range(2):
            send(src, dst, bs.at[p, d], br.at[p, d], xs[d])
        send(src, dst, bds.at[p, 0], bdr.at[p, 0], mate)
        dst[...] = src[...]

    def b_step(p):
        for d in range(2):
            src = b_rows(p, xfrom[d], core)
            arrived(src, bs.at[p, d], br.at[p, d])
            part = b_rows(p, xfrom[d], core, d * CHUNK, CHUNK)
            send(part, part, bfs.at[p, d], bfr.at[p, d], xs[d])
            send(src, src, bds.at[p, 1 + d], bdr.at[p, 1 + d], mate)

    def b_opp(p):
        for d in range(2):
            arrived(b_rows(p, wrap(x + 2), core, d * CHUNK, CHUNK), bfs.at[p, d], bfr.at[p, d])
        src = b_rows(p, wrap(x + 2), core)
        send(src, src, bds.at[p, 3], bdr.at[p, 3], mate)

    xrel = [x, xfrom[0], xfrom[1], wrap(x + 2)]

    def b_mate(p, i):
        arrived(b_rows(p, xrel[i], 1 - core), bds.at[p, i], bdr.at[p, i])

    def a_forward(k, kk, j):
        for d in range(2):
            arrived(a1.at[d, k, rows(j)], ys.at[d, kk, j], yr.at[d, k, j])
        src = a1.at[k, k, rows(j)]
        send(src, a1.at[2, k, rows(j)], yfs.at[k, j], yfr.at[k, j], dev(y_=wrap(y + 1 - 2 * k)))

    def a_opp(j):
        for d in range(2):
            arrived(a1.at[2, d, rows(j)], yfs.at[d, j], yfr.at[d, j])

    def ncols(n):
        return pl.ds(pl.multiple_of(n * NTILE, NTILE), NTILE)

    def m1_own(start, size):
        span = pl.ds(start, size)

        @pl.loop(0, COLS // NTILE)
        def _(n):
            for k in range(2):
                acc1[k, span, ncols(n)] = jnp.dot(
                    pz[2 * zl + k, span], s1[y, :, ncols(n)], preferred_element_type=jnp.float32)

    def m1(slot, yy, start, size):
        span = pl.ds(start, size)

        @pl.loop(0, COLS // NTILE)
        def _(n):
            for k in range(2):
                acc1[k, span, ncols(n)] += jnp.dot(
                    a1[slot, k, span], s1[yy, :, ncols(n)], preferred_element_type=jnp.float32)

    yrel = [wrap(y - 1), wrap(y + 1), wrap(y + 2)]

    def rs1_start(j):
        r1s[rows(j)] = acc1[1 - zl, rows(j)].astype(jnp.bfloat16)
        send(r1s.at[rows(j)], r1r.at[rows(j)], r1ss.at[j], r1rs.at[j], zp)

    def f_start(j):
        arrived(r1r.at[rows(j)], r1ss.at[j], r1rs.at[j])
        total = acc1[zl, rows(j)] + r1r[rows(j)].astype(jnp.float32)
        fa[0, rows(j)] = blocks_masked(total, fm_ref, j)
        for d in range(2):
            send(fa.at[0, rows(j)], fa.at[1 + d, rows(j)], fs.at[d, j], fr.at[d, j], yd[d])

    def f_forward(j):
        for d in range(2):
            arrived(fa.at[1 + d, rows(j)], fs.at[d, j], fr.at[d, j])
        d = j % 2
        send(fa.at[1 + d, rows(j)], fa.at[3, rows(j)], ffs.at[j], ffr.at[j], yd[d])

    def f_opp(j):
        arrived(fa.at[3, rows(j)], ffs.at[j], ffr.at[j])

    def diagonal(h):
        at = pl.multiple_of(core * ROWS + h * HALF, HALF)
        square = acc1[zh, rows(h, HALF), pl.ds(at, HALF)]
        r = lax.broadcasted_iota(jnp.int32, (HALF, HALF), 0)
        c = lax.broadcasted_iota(jnp.int32, (HALF, HALF), 1)
        return jnp.sum(jnp.where(r == c, square, 0.0))

    stages = [
        (core, 2, lambda i: dev(c_=lax.rem(core + i, 2))),
        (z, 4, lambda i: dev(z_=lax.rem(z + i, 4))),
        (y, 4, lambda i: dev(y_=lax.rem(y + i, 4))),
        (x, 4, lambda i: dev(x_=lax.rem(x + i, 4))),
    ]

    def e_send(st):
        me, n, target = stages[st]
        for i in range(1, n):
            send(eb.at[st, me], eb.at[st, me], es.at[st, i], er.at[st, i], target(i))

    def e_sum(st):
        me, n, _ = stages[st]
        for i in range(1, n):
            arrived(eb.at[st, lax.rem(me + n - i, n)], es.at[st, i], er.at[st, i])
        total = eb[st, 0]
        for i in range(1, n):
            total = total + eb[st, i]
        return total

    def e_step(st):
        total = e_sum(st)
        eb[st + 1, stages[st + 1][0]] = total
        e_send(st + 1)

    def m2(t, yy, slot, start, size, first):
        span = pl.ds(start, size)

        @pl.loop(0, COLS // NTILE)
        def _(n):
            d = jnp.dot(fa[slot, span], b2[t, yy, :, ncols(n)], preferred_element_type=jnp.float32)
            if first:
                acc2[t, span, ncols(n)] = d
            else:
                acc2[t, span, ncols(n)] += d

    def m2_half(h, xx, first):
        gap = wrap(xx - y)
        slot = jnp.where(gap == 0, 0, jnp.where(gap == 3, 1, jnp.where(gap == 1, 2, 3)))

        @pl.loop(0, COLS // NTILE)
        def _(n):
            d = jnp.zeros((ROWS, NTILE), jnp.float32)
            for c in range(2):
                at = pl.ds(c * ROWS + h * HALF, HALF)
                d += jnp.dot(fa[slot, :, at], b2[1, xx, at, ncols(n)], preferred_element_type=jnp.float32)
            if first:
                acc2[1, :, ncols(n)] = d
            else:
                acc2[1, :, ncols(n)] += d

    def rs2_start(j):
        r2s[rows(j)] = acc2[0, rows(j)].astype(jnp.bfloat16)
        send(r2s.at[rows(j)], r2r.at[rows(j)], r2ss.at[j], r2rs.at[j], z2)

    for j in (1, 2):
        p_mask(j)
    yb_step()
    n2_own(0)
    z_step(0)
    z_start(1)
    yb_opp()
    n2_far(0)
    z_step(1)
    z_start(2)
    n2_own(1)
    a_forward(k1, 0, 0)
    a_forward(k2, 1, 0)
    z_late(0)
    z_late(1)
    b_start(0)
    s_step(0)
    s_step(1)
    for i in range(3):
        yz_start_outer(i)
    n2_far(1)
    z_step(2)
    z_start(3)
    a_forward(k1, 0, 1)
    a_forward(k2, 1, 1)
    send_a(n1, k1, 0, 2)
    n2_own(2)
    z_step(3)
    for i in range(3):
        yz_start_inner(i)
    for i in range(3):
        yz_relay(i)
    n2_far(2)
    s_opp(0)
    s_opp(1)
    b_step(0)
    z_late(2)
    z_late(3)
    b_start(1)
    for i in range(4):
        for h in range(2):
            s_mate(i, h)
    m1_own(0, HALF)
    m1(0, yrel[0], 0, HALF)
    m1(1, yrel[1], 0, HALF)
    a_opp(0)
    a_opp(1)
    m1(2, yrel[2], 0, HALF)
    rs1_start(0)
    rs1_start(1)
    a_forward(k1, 0, 2)
    a_forward(k2, 1, 2)
    b_start(2)
    two, three = 2 * CHUNK, 3 * CHUNK
    m1_own(two, CHUNK)
    m1(0, yrel[0], two, CHUNK)
    m1(1, yrel[1], two, CHUNK)
    f_start(0)
    a_opp(2)
    m1(2, yrel[2], two, CHUNK)
    rs1_start(2)
    f_start(1)
    z_far(3)
    m1_own(three, CHUNK)
    for i in range(3):
        yz_arrived(i)
        m1(i, yrel[i], three, CHUNK)
    rs1_start(3)
    b_step(1)
    f_forward(0)
    f_start(2)
    trace = jnp.where(x == y, diagonal(0) + diagonal(1), 0.0)
    eb[0, core] = jnp.full((8, 128), trace, jnp.float32)
    e_send(0)
    f_forward(1)
    f_start(3)
    b_step(2)
    b_start(3)
    e_step(0)
    b_opp(0)
    b_opp(1)
    for p in range(2):
        for i in range(4):
            b_mate(p, i)
    f_forward(2)
    f_opp(0)
    f_opp(1)
    m2(0, y, 0, 0, HALF, True)
    for i in range(3):
        m2(0, yrel[i], 1 + i, 0, HALF, False)
    rs2_start(0)
    rs2_start(1)
    e_step(1)
    f_forward(3)
    m2(0, y, 0, two, CHUNK, True)
    for i in range(2):
        m2(0, yrel[i], 1 + i, two, CHUNK, False)
    f_opp(2)
    m2(0, yrel[2], 3, two, CHUNK, False)
    rs2_start(2)
    b_opp(2)
    b_step(3)
    m2(0, y, 0, three, CHUNK, True)
    for i in range(2):
        m2(0, yrel[i], 1 + i, three, CHUNK, False)
    e_step(2)
    f_opp(3)
    m2(0, yrel[2], 3, three, CHUNK, False)
    rs2_start(3)
    for h in range(2):
        if h == 1:
            b_opp(3)
        for i in range(4):
            b_mate(2 + h, i)
            m2_half(h, xrel[i], h == 0 and i == 0)
    e_ref[...] = e_sum(3)
    for j in range(4):
        arrived(r2r.at[rows(j)], r2ss.at[j], r2rs.at[j])
        total = acc2[1, rows(j)] + r2r[rows(j)].astype(jnp.float32)
        o_ref[rows(j)] = blocks_masked(total, fm_ref, j)
    for cp in sent:
        cp.wait_send()
    for i in range(3):
        yz_sent(i)
    for j in range(4):
        z_sent(j)


def shards(density, intersection, density_mask, intersection_mask, filter_mask):
    dma = pltpu.SemaphoreType.DMA
    bf16, f32 = jnp.bfloat16, jnp.float32
    vmem, smem = pl.BlockSpec(memory_space=pltpu.VMEM), pl.BlockSpec(memory_space=pltpu.SMEM)
    psp, electrons = pl.pallas_call(
        kernel,
        out_shape=(jax.ShapeDtypeStruct((ROWS, COLS), bf16), jax.ShapeDtypeStruct((8, 128), f32)),
        in_specs=[smem] * 3 + [vmem] * 2,
        out_specs=(vmem, vmem),
        scratch_shapes=[
            pltpu.VMEM((4, ROWS, COLS), bf16),
            pltpu.VMEM((3, CHUNK, COLS), bf16),
            pltpu.VMEM((3, CHUNK, COLS), bf16),
            pltpu.VMEM((3, 2, ROWS, COLS), bf16),
            pltpu.VMEM((4, 2 * ROWS, COLS), bf16),
            pltpu.VMEM((2, 4, 2 * ROWS, COLS), bf16),
            pltpu.VMEM((4, ROWS, COLS), bf16),
            pltpu.VMEM((2, ROWS, COLS), f32),
            pltpu.VMEM((2, ROWS, COLS), f32),
            pltpu.VMEM((ROWS, COLS), bf16),
            pltpu.VMEM((ROWS, COLS), bf16),
            pltpu.VMEM((ROWS, COLS), bf16),
            pltpu.VMEM((ROWS, COLS), bf16),
            pltpu.VMEM((4, 4, 8, 128), f32),
            dma((2, 4)), dma((2, 4)), dma((4,)), dma((4,)),
            dma((2, 2, 4)), dma((2, 2, 4)), dma((2, 4)), dma((2, 4)),
            dma((3,)), dma((3,)), dma((2, 3)), dma((2, 3)),
            dma((2, 2)), dma((2, 2)), dma((2, 2)), dma((2, 2)), dma((4, 2)), dma((4, 2)),
            dma((4, 2)), dma((4, 2)), dma((4, 2)), dma((4, 2)), dma((4, 4)), dma((4, 4)),
            dma((4,)), dma((4,)),
            dma((2, 4)), dma((2, 4)), dma((4,)), dma((4,)),
            dma((4,)), dma((4,)),
            dma((4, 4)), dma((4, 4)),
        ],
        compiler_params=pltpu.CompilerParams(
            collective_id=0, has_side_effects=True, vmem_limit_bytes=62 * 2**20
        ),
        cost_estimate=pl.CostEstimate(flops=17179869184, bytes_accessed=3 * 2**20, transcendentals=0),
    )(density_mask, intersection_mask, filter_mask, density, intersection)
    return psp, electrons[0, 0]


def solution(mesh):
    placed = (P("row", "col"),) * 5
    return jax.shard_map(
        shards, mesh=mesh, in_specs=placed, out_specs=(P("row", "col"), P()), check_vma=False
    )
```

time: 156 us -> 136 us (0.87)
  Pallas kernels: 152 us -> 132 us
    pallas_call x1, Pallas kernels: 152 us -> 132 us  [shards(): pl.pallas_call(kernel, out_shape=(jax.ShapeDtypeStruct((ROWS, COLS), bf16...]
where the time goes in v2:
time: 136 us
  Pallas kernels  132 us (97%)
  local copies, waits for them, and re-layouts  3.45 us (3%)
    pallas_call x1, Pallas kernels, shards(): pl.pallas_call(kernel, out_shape=(jax.ShapeDtypeStruct((ROWS, COLS), bf16...  132 us

profile of v2, /device:TPU:0, one launch (start us, length us, event | category | flops | bytes accessed | tf_op | source)
XLA Modules:
  0.0 135.9 jit_solution(3982598022254646915)
XLA Ops:
  0.6 131.8 %shard_map.68 = (bf16[512,1024]{1,0:T(8,128)(2,1)}, f32[8,128]{1,0:T(8,128)}) custom-call(s32[4,8]{1,0:T(4,128)} %dm_ref.1, s32[4,8]{1,0:T(4,128)} %im_ref.1, s32[4,8]{1,0:T(4,128)} %fm_ref.1, bf16[512,1024]{1,0:T(8,128)(2,1)} %p_ref.1, bf16[512,1024]{1,0:T(8,128)(2,1)} %s_ref.1), custom_call_target="tpu_custom_call" | custom-call | flops 17179869184 | bytes 3145728 | tf_op jit(solution)/shard_map/pallas_call | solution.py:558
  132.4 1.2 slice.3
  133.6 2.3 %copy.8 = bf16[512,1024]{1,0:T(8,128)(2,1)} copy(bf16[512,1024]{1,0:T(8,128)(2,1)} %get-tuple-element.8) | data formatting | bytes 2097152

commit v3 on v2

--- a/solution.py
+++ b/solution.py
@@ -10,7 +10,7 @@
 COLS = 1024
 CHUNK = 128
 HALF = 256
-NTILE = 256
+NTILE = 512
 MESH = pl.DeviceIdType.MESH
 
 
@@ -115,9 +115,6 @@
 
     def z_step(j):
         arrived(pz.at[n1, rows(j)], zs.at[0, j], zr.at[0, j])
-        if j < 2:
-            send_a(n1, k1, 0, j)
-
         @pl.when(inside)
         def _():
             arrived(pz.at[nl, rows(j)], zs.at[0, j], zr.at[1, j])
@@ -318,25 +315,24 @@
             arrived(a1.at[2, d, rows(j)], yfs.at[d, j], yfr.at[d, j])
 
     def ncols(n):
-        return pl.ds(pl.multiple_of(n * NTILE, NTILE), NTILE)
+        return pl.ds(n * NTILE, NTILE)
+
+    def m1_step(left, yy, start, size, first):
+        left = jnp.concatenate(left, axis=0)
+        for n in range(COLS // NTILE):
+            d = jnp.dot(left, s1[yy, :, ncols(n)], preferred_element_type=jnp.float32)
+            for k in range(2):
+                span, part = pl.ds(start, size), d[k * size:(k + 1) * size]
+                if first:
+                    acc1[k, span, ncols(n)] = part
+                else:
+                    acc1[k, span, ncols(n)] += part
 
     def m1_own(start, size):
-        span = pl.ds(start, size)
-
-        @pl.loop(0, COLS // NTILE)
-        def _(n):
-            for k in range(2):
-                acc1[k, span, ncols(n)] = jnp.dot(
-                    pz[2 * zl + k, span], s1[y, :, ncols(n)], preferred_element_type=jnp.float32)
+        m1_step([pz[2 * zl + k, pl.ds(start, size)] for k in range(2)], y, start, size, True)
 
     def m1(slot, yy, start, size):
-        span = pl.ds(start, size)
-
-        @pl.loop(0, COLS // NTILE)
-        def _(n):
-            for k in range(2):
-                acc1[k, span, ncols(n)] += jnp.dot(
-                    a1[slot, k, span], s1[yy, :, ncols(n)], preferred_element_type=jnp.float32)
+        m1_step([a1[slot, k, pl.ds(start, size)] for k in range(2)], yy, start, size, False)
 
     yrel = [wrap(y - 1), wrap(y + 1), wrap(y + 2)]
 
@@ -396,8 +392,7 @@
     def m2(t, yy, slot, start, size, first):
         span = pl.ds(start, size)
 
-        @pl.loop(0, COLS // NTILE)
-        def _(n):
+        for n in range(COLS // NTILE):
             d = jnp.dot(fa[slot, span], b2[t, yy, :, ncols(n)], preferred_element_type=jnp.float32)
             if first:
                 acc2[t, span, ncols(n)] = d
@@ -408,8 +403,7 @@
         gap = wrap(xx - y)
         slot = jnp.where(gap == 0, 0, jnp.where(gap == 3, 1, jnp.where(gap == 1, 2, 3)))
 
-        @pl.loop(0, COLS // NTILE)
-        def _(n):
+        for n in range(COLS // NTILE):
             d = jnp.zeros((ROWS, NTILE), jnp.float32)
             for c in range(2):
                 at = pl.ds(c * ROWS + h * HALF, HALF)
@@ -425,120 +419,128 @@
 
     for j in (1, 2):
         p_mask(j)
+    two, three = 2 * CHUNK, 3 * CHUNK
+    z_start(1)
     yb_step()
-    n2_own(0)
     z_step(0)
-    z_start(1)
+    send_a(n1, k1, 0, 0)
+    z_step(1)
+    z_late(0)
+    z_start(2)
+    send_a(n1, k1, 0, 1)
     yb_opp()
-    n2_far(0)
-    z_step(1)
-    z_start(2)
-    n2_own(1)
-    a_forward(k1, 0, 0)
-    a_forward(k2, 1, 0)
-    z_late(0)
-    z_late(1)
-    b_start(0)
-    s_step(0)
-    s_step(1)
+    z_start(3)
     for i in range(3):
         yz_start_outer(i)
+    n2_far(0)
+    s_step(0)
+    n2_own(0)
     n2_far(1)
+    s_step(1)
+    z_late(1)
+    n2_own(1)
     z_step(2)
-    z_start(3)
-    a_forward(k1, 0, 1)
-    a_forward(k2, 1, 1)
-    send_a(n1, k1, 0, 2)
-    n2_own(2)
+    a_forward(k2, 1, 0)
+    a_forward(k1, 0, 0)
+    b_start(2)
+    s_opp(1)
     z_step(3)
     for i in range(3):
         yz_start_inner(i)
+    s_opp(0)
+    a_forward(k1, 0, 1)
+    a_forward(k2, 1, 1)
     for i in range(3):
         yz_relay(i)
+    b_start(0)
+    z_late(2)
     n2_far(2)
-    s_opp(0)
-    s_opp(1)
-    b_step(0)
-    z_late(2)
-    z_late(3)
-    b_start(1)
+    n2_own(2)
     for i in range(4):
         for h in range(2):
             s_mate(i, h)
+    z_far(3)
+    a_opp(0)
     m1_own(0, HALF)
+    z_late(3)
+    a_opp(1)
+    send_a(n1, k1, 0, 2)
+    b_start(1)
+    m1(2, yrel[2], 0, HALF)
     m1(0, yrel[0], 0, HALF)
     m1(1, yrel[1], 0, HALF)
-    a_opp(0)
-    a_opp(1)
-    m1(2, yrel[2], 0, HALF)
     rs1_start(0)
+    a_forward(k2, 1, 2)
+    a_forward(k1, 0, 2)
     rs1_start(1)
-    a_forward(k1, 0, 2)
-    a_forward(k2, 1, 2)
-    b_start(2)
-    two, three = 2 * CHUNK, 3 * CHUNK
     m1_own(two, CHUNK)
     m1(0, yrel[0], two, CHUNK)
     m1(1, yrel[1], two, CHUNK)
     f_start(0)
+    f_start(1)
     a_opp(2)
+    m1_own(three, CHUNK)
+    b_step(0)
     m1(2, yrel[2], two, CHUNK)
     rs1_start(2)
-    f_start(1)
-    z_far(3)
-    m1_own(three, CHUNK)
+    b_step(1)
+    b_step(2)
     for i in range(3):
         yz_arrived(i)
         m1(i, yrel[i], three, CHUNK)
+    f_forward(0)
+    f_forward(1)
+    f_start(2)
     rs1_start(3)
-    b_step(1)
-    f_forward(0)
-    f_start(2)
     trace = jnp.where(x == y, diagonal(0) + diagonal(1), 0.0)
     eb[0, core] = jnp.full((8, 128), trace, jnp.float32)
     e_send(0)
-    f_forward(1)
+    b_start(3)
+    b_opp(0)
+    for i in range(4):
+        b_mate(0, i)
+    e_step(0)
+    f_opp(0)
+    b_opp(1)
     f_start(3)
-    b_step(2)
-    b_start(3)
-    e_step(0)
-    b_opp(0)
-    b_opp(1)
-    for p in range(2):
-        for i in range(4):
-            b_mate(p, i)
+    f_opp(1)
+    for i in range(4):
+        b_mate(1, i)
+    m2(0, y, 0, 0, HALF, True)
+    for i in range(2):
+        m2(0, yrel[i], 1 + i, 0, HALF, False)
+    m2(0, yrel[2], 3, 0, HALF, False)
+    rs2_start(1)
     f_forward(2)
-    f_opp(0)
-    f_opp(1)
-    m2(0, y, 0, 0, HALF, True)
-    for i in range(3):
-        m2(0, yrel[i], 1 + i, 0, HALF, False)
     rs2_start(0)
-    rs2_start(1)
+    f_forward(3)
+    b_opp(2)
     e_step(1)
-    f_forward(3)
+    m2(0, y, 0, three, CHUNK, True)
+    for i in range(2):
+        m2(0, yrel[i], 1 + i, three, CHUNK, False)
     m2(0, y, 0, two, CHUNK, True)
     for i in range(2):
         m2(0, yrel[i], 1 + i, two, CHUNK, False)
     f_opp(2)
     m2(0, yrel[2], 3, two, CHUNK, False)
     rs2_start(2)
-    b_opp(2)
+    f_opp(3)
     b_step(3)
-    m2(0, y, 0, three, CHUNK, True)
-    for i in range(2):
-        m2(0, yrel[i], 1 + i, three, CHUNK, False)
+    for i in range(4):
+        b_mate(2, i)
+    for i in range(4):
+        m2_half(0, xrel[i], i == 0)
     e_step(2)
-    f_opp(3)
     m2(0, yrel[2], 3, three, CHUNK, False)
     rs2_start(3)
-    for h in range(2):
-        if h == 1:
-            b_opp(3)
-        for i in range(4):
-            b_mate(2 + h, i)
-            m2_half(h, xrel[i], h == 0 and i == 0)
-    e_ref[...] = e_sum(3)
+    for i in range(3):
+        b_mate(3, i)
+        m2_half(1, xrel[i], False)
+    b_opp(3)
+    b_mate(3, 3)
+    m2_half(1, xrel[3], False)
+    e_ref[0, 0] = jnp.max(e_sum(3))
     for j in range(4):
         arrived(r2r.at[rows(j)], r2ss.at[j], r2rs.at[j])
         total = acc2[1, rows(j)] + r2r[rows(j)].astype(jnp.float32)
@@ -557,9 +559,9 @@
     vmem, smem = pl.BlockSpec(memory_space=pltpu.VMEM), pl.BlockSpec(memory_space=pltpu.SMEM)
     psp, electrons = pl.pallas_call(
         kernel,
-        out_shape=(jax.ShapeDtypeStruct((ROWS, COLS), bf16), jax.ShapeDtypeStruct((8, 128), f32)),
+        out_shape=(jax.ShapeDtypeStruct((ROWS, COLS), bf16), jax.ShapeDtypeStruct((1, 1), f32)),
         in_specs=[smem] * 3 + [vmem] * 2,
-        out_specs=(vmem, vmem),
+        out_specs=(vmem, smem),
         scratch_shapes=[
             pltpu.VMEM((4, ROWS, COLS), bf16),
             pltpu.VMEM((3, CHUNK, COLS), bf16),
@@ -590,7 +592,7 @@
         ),
         cost_estimate=pl.CostEstimate(flops=17179869184, bytes_accessed=3 * 2**20, transcendentals=0),
     )(density_mask, intersection_mask, filter_mask, density, intersection)
-    return psp, electrons[0, 0]
+    return psp, electrons.reshape(())
 
 
 def solution(mesh):

time: 136 us -> 128 us (0.941)
  Pallas kernels: 132 us -> 122 us
  between operations: 0.64 us -> 2.33 us
    pallas_call x1, Pallas kernels: 132 us -> 122 us  [shards(): pl.pallas_call(kernel, out_shape=(jax.ShapeDtypeStruct((ROWS, COLS), bf16...]
where the time goes in v3:
time: 128 us; the launch traced here: 127 us
  Pallas kernels  122 us (95%)
  between operations  2.33 us (2%)
  local copies, waits for them, and re-layouts  2.26 us (2%)
    pallas_call x1, Pallas kernels, shards(): pl.pallas_call(kernel, out_shape=(jax.ShapeDtypeStruct((ROWS, COLS), bf16...  122 us

profile of v3, /device:TPU:0, one launch (start us, length us, event | category | flops | bytes accessed | tf_op | source)
XLA Modules:
  0.0 127.0 jit_solution(5198525288950508412)
XLA Ops:
  0.6 122.4 %shard_map.68 = (bf16[512,1024]{1,0:T(8,128)(2,1)}, f32[1,1]{1,0:T(1,128)}) custom-call(s32[4,8]{1,0:T(4,128)} %dm_ref.1, s32[4,8]{1,0:T(4,128)} %im_ref.1, s32[4,8]{1,0:T(4,128)} %fm_ref.1, bf16[512,1024]{1,0:T(8,128)(2,1)} %p_ref.1, bf16[512,1024]{1,0:T(8,128)(2,1)} %s_ref.1), custom_call_target="tpu_custom_call" | custom-call | flops 17179869184 | bytes 3145728 | tf_op jit(solution)/shard_map/pallas_call | solution.py:560
  123.0 2.3 %copy.9 = bf16[512,1024]{1,0:T(8,128)(2,1)} copy(bf16[512,1024]{1,0:T(8,128)(2,1)} %get-tuple-element.8) | data formatting | bytes 2097152

commit v4 on v3

--- a/solution.py
+++ b/solution.py
@@ -15,11 +15,20 @@
 
 
 def kernel(
-    dm_ref, im_ref, fm_ref, p_ref, s_ref, o_ref, e_ref,
-    pz, yb, yf, a1, s1, b2, fa, acc1, acc2, r1s, r1r, r2s, r2r, eb,
+    dm_ref, im_ref, fm_ref, p_hbm, s_hbm, o_hbm, e_ref,
+    p_ref, s_ref, o_ref, pz, yb, yf, a1, s1, b2, fa, acc1, acc2, r1s, r1r, r2s, r2r, eb,
     zs, zr, zfs, zfr, ys, yr, yfs, yfr, ybs, ybr, yzs, yzr, ss, sr, sfs, sfr, sds, sdr,
-    bs, br, bfs, bfr, bds, bdr, r1ss, r1rs, fs, fr, ffs, ffr, r2ss, r2rs, es, er,
+    bs, br, bfs, bfr, bds, bdr, r1ss, r1rs, fs, fr, ffs, ffr, r2ss, r2rs, es, er, ps, sl, os,
 ):
+    def load(hbm, ref, sems, j):
+        span = pl.ds(j * CHUNK, CHUNK)
+        return pltpu.make_async_copy(hbm.at[span], ref.at[span], sems.at[j])
+
+    for j in (3, 0, 1, 2):
+        load(p_hbm, p_ref, ps, j).start()
+    for j in range(4):
+        load(s_hbm, s_ref, sl, j).start()
+
     row = lax.axis_index("row")
     col = lax.axis_index("col")
     core = lax.rem(row, 2)
@@ -49,7 +58,7 @@
         pl.semaphore_signal(barrier, inc=1, device_id=d, device_id_type=MESH)
     pl.semaphore_wait(barrier, len(peers))
 
-    sent = []
+    sent, late = [], []
 
     def copy(src, dst, ssem, rsem, device):
         return pltpu.make_async_remote_copy(
@@ -232,6 +241,7 @@
                 cp.wait_send()
 
     def p_mask(j):
+        load(p_hbm, p_ref, ps, j).wait()
         pz[z, rows(j)] = blocks_masked(p_ref[rows(j)], dm_ref, j)
 
     p_mask(LAST)
@@ -245,6 +255,7 @@
     for h in range(2):
         for i in range(2):
             j = 2 * h + i
+            load(s_hbm, s_ref, sl, j).wait()
             s1[x, pl.ds(pl.multiple_of(core * ROWS + j * CHUNK, CHUNK), CHUNK)] = blocks_masked(
                 s_ref[rows(j)], im_ref, j)
         src = s_piece(x, core, h)
@@ -416,6 +427,7 @@
     def rs2_start(j):
         r2s[rows(j)] = acc2[0, rows(j)].astype(jnp.bfloat16)
         send(r2s.at[rows(j)], r2r.at[rows(j)], r2ss.at[j], r2rs.at[j], z2)
+        late.append(sent.pop())
 
     for j in (1, 2):
         p_mask(j)
@@ -541,10 +553,6 @@
     b_mate(3, 3)
     m2_half(1, xrel[3], False)
     e_ref[0, 0] = jnp.max(e_sum(3))
-    for j in range(4):
-        arrived(r2r.at[rows(j)], r2ss.at[j], r2rs.at[j])
-        total = acc2[1, rows(j)] + r2r[rows(j)].astype(jnp.float32)
-        o_ref[rows(j)] = blocks_masked(total, fm_ref, j)
     for cp in sent:
         cp.wait_send()
     for i in range(3):
@@ -552,17 +560,47 @@
     for j in range(4):
         z_sent(j)
 
+    def store(j):
+        return pltpu.make_async_copy(o_ref.at[rows(j)], o_hbm.at[rows(j)], os.at[j])
+
+    for j in range(4):
+        arrived(r2r.at[rows(j)], r2ss.at[j], r2rs.at[j])
+        total = acc2[1, rows(j)] + r2r[rows(j)].astype(jnp.float32)
+        o_ref[rows(j)] = blocks_masked(total, fm_ref, j)
+        store(j).start()
+    for cp in late:
+        cp.wait_send()
+    for j in range(4):
+        store(j).wait()
+
+
+def place(psp_ref, trace_ref, to_ref, to_trace_ref, held, in_sems, out_sems):
+    spans = [pl.ds(i * 64, 64) for i in range(8)]
+    loads = [pltpu.make_async_copy(psp_ref.at[s], held.at[s], in_sems.at[i]) for i, s in enumerate(spans)]
+    stores = [pltpu.make_async_copy(held.at[s], to_ref.at[s], out_sems.at[i]) for i, s in enumerate(spans)]
+    for cp in loads:
+        cp.start()
+    to_trace_ref[0, 0] = trace_ref[0, 0]
+    for load, store in zip(loads, stores):
+        load.wait()
+        store.start()
+    for cp in stores:
+        cp.wait()
+
 
 def shards(density, intersection, density_mask, intersection_mask, filter_mask):
     dma = pltpu.SemaphoreType.DMA
     bf16, f32 = jnp.bfloat16, jnp.float32
-    vmem, smem = pl.BlockSpec(memory_space=pltpu.VMEM), pl.BlockSpec(memory_space=pltpu.SMEM)
+    hbm, smem = pl.BlockSpec(memory_space=pl.ANY), pl.BlockSpec(memory_space=pltpu.SMEM)
     psp, electrons = pl.pallas_call(
         kernel,
         out_shape=(jax.ShapeDtypeStruct((ROWS, COLS), bf16), jax.ShapeDtypeStruct((1, 1), f32)),
-        in_specs=[smem] * 3 + [vmem] * 2,
-        out_specs=(vmem, smem),
+        in_specs=[smem] * 3 + [hbm] * 2,
+        out_specs=(hbm, smem),
         scratch_shapes=[
+            pltpu.VMEM((ROWS, COLS), bf16),
+            pltpu.VMEM((ROWS, COLS), bf16),
+            pltpu.VMEM((ROWS, COLS), bf16),
             pltpu.VMEM((4, ROWS, COLS), bf16),
             pltpu.VMEM((3, CHUNK, COLS), bf16),
             pltpu.VMEM((3, CHUNK, COLS), bf16),
@@ -586,12 +624,20 @@
             dma((2, 4)), dma((2, 4)), dma((4,)), dma((4,)),
             dma((4,)), dma((4,)),
             dma((4, 4)), dma((4, 4)),
+            dma((4,)), dma((4,)), dma((4,)),
         ],
         compiler_params=pltpu.CompilerParams(
             collective_id=0, has_side_effects=True, vmem_limit_bytes=62 * 2**20
         ),
         cost_estimate=pl.CostEstimate(flops=17179869184, bytes_accessed=3 * 2**20, transcendentals=0),
     )(density_mask, intersection_mask, filter_mask, density, intersection)
+    psp, electrons = pl.pallas_call(
+        place,
+        out_shape=(jax.ShapeDtypeStruct((ROWS, COLS), bf16), jax.ShapeDtypeStruct((1, 1), f32)),
+        in_specs=[hbm, smem],
+        out_specs=(hbm, smem),
+        scratch_shapes=[pltpu.VMEM((ROWS, COLS), bf16), dma((8,)), dma((8,))],
+    )(psp, electrons)
     return psp, electrons.reshape(())
 
 

time: 128 us -> 127 us (level)
  Pallas kernels: 122 us -> 125 us
  local copies, waits for them, and re-layouts: 2.26 us -> 0 us
  between operations: 2.33 us -> 0.64 us
    pallas_call x0 -> x1, Pallas kernels: none -> 3.23 us  [shards(): pl.pallas_call(place, out_shape=(jax.ShapeDtypeStruct((ROWS, COLS), bf16)...]
    unnamed x1 -> x0, local copies, waits for them, and re-layouts: 2.26 us -> none
where the time goes in v4:
time: 127 us; the launch traced here: 126 us
  Pallas kernels  125 us (98%)
    pallas_call x1, Pallas kernels, shards(): pl.pallas_call(kernel, out_shape=(jax.ShapeDtypeStruct((ROWS, COLS), bf16...  122 us
    pallas_call x1, Pallas kernels, shards(): pl.pallas_call(place, out_shape=(jax.ShapeDtypeStruct((ROWS, COLS), bf16)...  3.23 us

profile of v4, /device:TPU:0, one launch (start us, length us, event | category | flops | bytes accessed | tf_op | source)
XLA Modules:
  0.0 125.6 jit_solution(9893099450028597985)
XLA Ops:
  0.6 121.7 %shard_map.68 = (bf16[512,1024]{1,0:T(8,128)(2,1)}, f32[1,1]{1,0:T(1,128)}) custom-call(s32[4,8]{1,0:T(4,128)} %dm_ref.1, s32[4,8]{1,0:T(4,128)} %im_ref.1, s32[4,8]{1,0:T(4,128)} %fm_ref.1, bf16[512,1024]{1,0:T(8,128)(2,1)} %p_hbm.1, bf16[512,1024]{1,0:T(8,128)(2,1)} %s_hbm.1), custom_call_target="tpu_custom_call" | custom-call | flops 17179869184 | bytes 3145728 | tf_op jit(solution)/shard_map/pallas_call | solution.py:595
  122.3 3.2 %shard_map.69 = (bf16[512,1024]{1,0:T(8,128)(2,1)}, f32[1,1]{1,0:T(1,128)}) custom-call(bf16[512,1024]{1,0:T(8,128)(2,1)} %get-tuple-element.6.psp_ref, f32[1,1]{1,0:T(1,128)} %get-tuple-element.7.trace_ref), custom_call_target="tpu_custom_call" | custom-call | tf_op jit(solution)/shard_map/pallas_call | solution.py:634

commit v5 on v4

--- a/solution.py
+++ b/solution.py
@@ -433,88 +433,87 @@
         p_mask(j)
     two, three = 2 * CHUNK, 3 * CHUNK
     z_start(1)
+    n2_own(0)
     yb_step()
     z_step(0)
     send_a(n1, k1, 0, 0)
     z_step(1)
+    send_a(n1, k1, 0, 1)
+    n2_far(0)
+    s_step(0)
+    z_start(2)
+    n2_own(1)
     z_late(0)
-    z_start(2)
-    send_a(n1, k1, 0, 1)
     yb_opp()
-    z_start(3)
     for i in range(3):
         yz_start_outer(i)
-    n2_far(0)
-    s_step(0)
-    n2_own(0)
+    z_start(3)
     n2_far(1)
     s_step(1)
-    z_late(1)
-    n2_own(1)
-    z_step(2)
     a_forward(k2, 1, 0)
     a_forward(k1, 0, 0)
     b_start(2)
-    s_opp(1)
+    z_step(2)
+    s_opp(0)
+    a_forward(k2, 1, 1)
     z_step(3)
+    a_forward(k1, 0, 1)
     for i in range(3):
         yz_start_inner(i)
-    s_opp(0)
-    a_forward(k1, 0, 1)
-    a_forward(k2, 1, 1)
+    z_late(1)
     for i in range(3):
         yz_relay(i)
+    s_opp(1)
     b_start(0)
-    z_late(2)
-    n2_far(2)
     n2_own(2)
+    send_a(n1, k1, 0, 2)
     for i in range(4):
         for h in range(2):
             s_mate(i, h)
-    z_far(3)
+    m1_own(0, HALF)
     a_opp(0)
-    m1_own(0, HALF)
-    z_late(3)
     a_opp(1)
-    send_a(n1, k1, 0, 2)
-    b_start(1)
-    m1(2, yrel[2], 0, HALF)
+    z_late(2)
+    n2_far(2)
     m1(0, yrel[0], 0, HALF)
     m1(1, yrel[1], 0, HALF)
+    m1(2, yrel[2], 0, HALF)
     rs1_start(0)
+    z_late(3)
+    z_far(3)
+    rs1_start(1)
+    m1_own(three, CHUNK)
+    b_start(1)
+    a_forward(k1, 0, 2)
     a_forward(k2, 1, 2)
-    a_forward(k1, 0, 2)
-    rs1_start(1)
     m1_own(two, CHUNK)
-    m1(0, yrel[0], two, CHUNK)
-    m1(1, yrel[1], two, CHUNK)
     f_start(0)
-    f_start(1)
-    a_opp(2)
-    m1_own(three, CHUNK)
-    b_step(0)
-    m1(2, yrel[2], two, CHUNK)
-    rs1_start(2)
-    b_step(1)
-    b_step(2)
     for i in range(3):
         yz_arrived(i)
         m1(i, yrel[i], three, CHUNK)
+    a_opp(2)
+    rs1_start(3)
+    m1(2, yrel[2], two, CHUNK)
+    f_start(1)
+    b_step(0)
+    m1(0, yrel[0], two, CHUNK)
+    m1(1, yrel[1], two, CHUNK)
+    b_step(1)
     f_forward(0)
-    f_forward(1)
-    f_start(2)
-    rs1_start(3)
+    rs1_start(2)
     trace = jnp.where(x == y, diagonal(0) + diagonal(1), 0.0)
     eb[0, core] = jnp.full((8, 128), trace, jnp.float32)
     e_send(0)
+    f_forward(1)
+    e_step(0)
+    b_opp(0)
+    f_start(2)
+    b_opp(1)
     b_start(3)
-    b_opp(0)
+    f_opp(0)
+    f_start(3)
     for i in range(4):
         b_mate(0, i)
-    e_step(0)
-    f_opp(0)
-    b_opp(1)
-    f_start(3)
     f_opp(1)
     for i in range(4):
         b_mate(1, i)
@@ -522,34 +521,35 @@
     for i in range(2):
         m2(0, yrel[i], 1 + i, 0, HALF, False)
     m2(0, yrel[2], 3, 0, HALF, False)
+    rs2_start(0)
     rs2_start(1)
     f_forward(2)
-    rs2_start(0)
+    m2(0, y, 0, two, CHUNK, True)
+    for i in range(2):
+        m2(0, yrel[i], 1 + i, two, CHUNK, False)
+    b_step(2)
     f_forward(3)
-    b_opp(2)
-    e_step(1)
+    f_opp(2)
+    m2(0, yrel[2], 3, two, CHUNK, False)
+    rs2_start(2)
+    b_step(3)
     m2(0, y, 0, three, CHUNK, True)
     for i in range(2):
         m2(0, yrel[i], 1 + i, three, CHUNK, False)
-    m2(0, y, 0, two, CHUNK, True)
-    for i in range(2):
-        m2(0, yrel[i], 1 + i, two, CHUNK, False)
-    f_opp(2)
-    m2(0, yrel[2], 3, two, CHUNK, False)
-    rs2_start(2)
+    e_step(1)
+    b_opp(2)
     f_opp(3)
-    b_step(3)
+    m2(0, yrel[2], 3, three, CHUNK, False)
+    rs2_start(3)
+    e_step(2)
     for i in range(4):
         b_mate(2, i)
     for i in range(4):
         m2_half(0, xrel[i], i == 0)
-    e_step(2)
-    m2(0, yrel[2], 3, three, CHUNK, False)
-    rs2_start(3)
+    b_opp(3)
     for i in range(3):
         b_mate(3, i)
         m2_half(1, xrel[i], False)
-    b_opp(3)
     b_mate(3, 3)
     m2_half(1, xrel[3], False)
     e_ref[0, 0] = jnp.max(e_sum(3))

time: 127 us -> 125 us (0.984); the launches traced: 126 us -> 125 us
  no operation moved by 1% of the time
where the time goes in v5:
time: 125 us
  Pallas kernels  125 us (100%)
    pallas_call x1, Pallas kernels, shards(): pl.pallas_call(kernel, out_shape=(jax.ShapeDtypeStruct((ROWS, COLS), bf16...  121 us
    pallas_call x1, Pallas kernels, shards(): pl.pallas_call(place, out_shape=(jax.ShapeDtypeStruct((ROWS, COLS), bf16)...  3.23 us

profile of v5, /device:TPU:0, one launch (start us, length us, event | category | flops | bytes accessed | tf_op | source)
XLA Modules:
  0.0 125.3 jit_solution(2799755415926323282)
XLA Ops:
  0.6 121.4 %shard_map.68 = (bf16[512,1024]{1,0:T(8,128)(2,1)}, f32[1,1]{1,0:T(1,128)}) custom-call(s32[4,8]{1,0:T(4,128)} %dm_ref.1, s32[4,8]{1,0:T(4,128)} %im_ref.1, s32[4,8]{1,0:T(4,128)} %fm_ref.1, bf16[512,1024]{1,0:T(8,128)(2,1)} %p_hbm.1, bf16[512,1024]{1,0:T(8,128)(2,1)} %s_hbm.1), custom_call_target="tpu_custom_call" | custom-call | flops 17179869184 | bytes 3145728 | tf_op jit(solution)/shard_map/pallas_call | solution.py:595
  122.0 3.2 %shard_map.69 = (bf16[512,1024]{1,0:T(8,128)(2,1)}, f32[1,1]{1,0:T(1,128)}) custom-call(bf16[512,1024]{1,0:T(8,128)(2,1)} %get-tuple-element.6.psp_ref, f32[1,1]{1,0:T(1,128)} %get-tuple-element.7.trace_ref), custom_call_target="tpu_custom_call" | custom-call | tf_op jit(solution)/shard_map/pallas_call | solution.py:634

commit v6 on v5

--- a/solution.py
+++ b/solution.py
@@ -10,7 +10,7 @@
 COLS = 1024
 CHUNK = 128
 HALF = 256
-NTILE = 512
+NTILE = 1024
 MESH = pl.DeviceIdType.MESH
 
 
@@ -494,13 +494,13 @@
     a_opp(2)
     rs1_start(3)
     m1(2, yrel[2], two, CHUNK)
+    m1(0, yrel[0], two, CHUNK)
+    m1(1, yrel[1], two, CHUNK)
+    rs1_start(2)
     f_start(1)
     b_step(0)
-    m1(0, yrel[0], two, CHUNK)
-    m1(1, yrel[1], two, CHUNK)
     b_step(1)
     f_forward(0)
-    rs1_start(2)
     trace = jnp.where(x == y, diagonal(0) + diagonal(1), 0.0)
     eb[0, core] = jnp.full((8, 128), trace, jnp.float32)
     e_send(0)
@@ -529,6 +529,7 @@
         m2(0, yrel[i], 1 + i, two, CHUNK, False)
     b_step(2)
     f_forward(3)
+    e_step(1)
     f_opp(2)
     m2(0, yrel[2], 3, two, CHUNK, False)
     rs2_start(2)
@@ -536,11 +537,10 @@
     m2(0, y, 0, three, CHUNK, True)
     for i in range(2):
         m2(0, yrel[i], 1 + i, three, CHUNK, False)
-    e_step(1)
-    b_opp(2)
     f_opp(3)
     m2(0, yrel[2], 3, three, CHUNK, False)
     rs2_start(3)
+    b_opp(2)
     e_step(2)
     for i in range(4):
         b_mate(2, i)

time: 125 us -> 125 us (level)
  no operation moved by 1% of the time
where the time goes in v6:
time: 125 us
  Pallas kernels  125 us (100%)
    pallas_call x1, Pallas kernels, shards(): pl.pallas_call(kernel, out_shape=(jax.ShapeDtypeStruct((ROWS, COLS), bf16...  121 us
    pallas_call x1, Pallas kernels, shards(): pl.pallas_call(place, out_shape=(jax.ShapeDtypeStruct((ROWS, COLS), bf16)...  3.23 us

profile of v6, /device:TPU:0, one launch (start us, length us, event | category | flops | bytes accessed | tf_op | source)
XLA Modules:
  0.0 125.3 jit_solution(11599911437045589575)
XLA Ops:
  0.6 121.4 %shard_map.68 = (bf16[512,1024]{1,0:T(8,128)(2,1)}, f32[1,1]{1,0:T(1,128)}) custom-call(s32[4,8]{1,0:T(4,128)} %dm_ref.1, s32[4,8]{1,0:T(4,128)} %im_ref.1, s32[4,8]{1,0:T(4,128)} %fm_ref.1, bf16[512,1024]{1,0:T(8,128)(2,1)} %p_hbm.1, bf16[512,1024]{1,0:T(8,128)(2,1)} %s_hbm.1), custom_call_target="tpu_custom_call" | custom-call | flops 17179869184 | bytes 3145728 | tf_op jit(solution)/shard_map/pallas_call | solution.py:595
  122.0 3.2 %shard_map.69 = (bf16[512,1024]{1,0:T(8,128)(2,1)}, f32[1,1]{1,0:T(1,128)}) custom-call(bf16[512,1024]{1,0:T(8,128)(2,1)} %get-tuple-element.6.psp_ref, f32[1,1]{1,0:T(1,128)} %get-tuple-element.7.trace_ref), custom_call_target="tpu_custom_call" | custom-call | tf_op jit(solution)/shard_map/pallas_call | solution.py:634
